TPU v7x, 32 devices: a whole 2x2x4 slice. The times are simulated.
32 devices in a mesh: groups: 2 (over y), frame: 4 (over x, core), space: 4 (over z).
Axes of the slice: x: 2, y: 2, z: 4, core: 2. Of those that a mesh axis runs over, the one named last changes fastest.
Arguments:
- tokens: bfloat16 [16, 512, 1024], P(('groups', 'frame'), 'space'), parts along dimension 0, may hold values from -40 to 40
- norm_gain: float32 [1024], replicated, may hold values from 0.1 to 1.9
- w_query: bfloat16 [1024, 1024], P(('frame', 'space')), may hold values from -1 to 1
- w_key: bfloat16 [1024, 1024], P(('frame', 'space')), may hold values from -1 to 1
- w_value: bfloat16 [1024, 1024], P(('frame', 'space')), may hold values from -0.1875 to 0.1875
- w_output: bfloat16 [1024, 1024], P(('frame', 'space')), may hold values from -0.1875 to 0.1875
- grad_out: bfloat16 [16, 512, 1024], P(('groups', 'frame'), 'space'), parts along dimension 0, may hold values from -6 to 6
Outputs:
- grad_in: bfloat16 [16, 512, 1024], P(('groups', 'frame'), 'space'), parts along dimension 0
There are 2 independent parts, one for each index of `groups`. A program takes and returns all parts, laid end to end along the dimension named above; an argument that names none is the same for every part. Nothing has to cross between parts.
All inputs are finite; a program needn't handle non-finite values.
Results may differ from a plain program's by a relative error of at most 0.006.
The roundings to bfloat16 on the way count: a program that leaves them out, or rounds other values in their place, can miss the bound.
Values may be sent and summed in bfloat16 or wider, within the bound.
A program may use at most 64 MiB of HBM per device.

v0:
```python
import jax
import jax.numpy as jnp
from jax import lax
from jax.sharding import PartitionSpec as P

HEADS = 16


norm_epsilon = 1e-05


def normalize(tokens, norm_gain):
    values = tokens.astype(jnp.float32)
    centred = values - jnp.mean(values, axis=-1, keepdims=True)
    inverse = lax.rsqrt(jnp.mean(centred * centred, axis=-1, keepdims=True) + norm_epsilon)
    unit = centred * inverse
    return ((unit * norm_gain).astype(jnp.bfloat16), unit, inverse)


def project(source, weight):
    flat = source.reshape(-1, source.shape[-1])
    result = jnp.dot(flat, weight, preferred_element_type=jnp.float32)
    return result.reshape(source.shape[:-1] + (weight.shape[1],))


def project_back(source, weight):
    flat = source.reshape(-1, source.shape[-1])
    result = lax.dot_general(
        flat, weight, (((1,), (1,)), ((), ())), preferred_element_type=jnp.float32
    )
    return result.reshape(source.shape[:-1] + (weight.shape[0],))


def split_heads(source):
    return source.reshape(source.shape[0], source.shape[1], HEADS, -1)


def join_heads(source):
    return source.reshape(source.shape[0], source.shape[1], -1)


def attend_back(query_heads, key_heads, value_heads, grad_heads):
    scaling = query_heads.shape[3] ** (-0.5)
    scores = (
        jnp.einsum("fphd,gphd->phfg", query_heads, key_heads, preferred_element_type=jnp.float32)
        * scaling
    )
    scores = scores - jnp.max(scores, axis=-1, keepdims=True)
    expo = jnp.exp(scores)
    attn_probs = expo / jnp.sum(expo, axis=-1, keepdims=True)
    probs_low = attn_probs.astype(jnp.bfloat16)
    grad_value = jnp.einsum(
        "phfg,fphd->gphd", probs_low, grad_heads, preferred_element_type=jnp.float32
    ).astype(jnp.bfloat16)
    grad_probs = jnp.einsum(
        "fphd,gphd->phfg", grad_heads, value_heads, preferred_element_type=jnp.float32
    )
    row_inner = jnp.sum(attn_probs * grad_probs, axis=-1, keepdims=True)
    grad_scores = (attn_probs * (grad_probs - row_inner) * scaling).astype(jnp.bfloat16)
    grad_query = jnp.einsum(
        "phfg,gphd->fphd", grad_scores, key_heads, preferred_element_type=jnp.float32
    ).astype(jnp.bfloat16)
    grad_key = jnp.einsum(
        "phfg,fphd->gphd", grad_scores, query_heads, preferred_element_type=jnp.float32
    ).astype(jnp.bfloat16)
    return (grad_query, grad_key, grad_value)


def norm_back(grad_out, grad_normed, unit, inverse, norm_gain):
    scaled = grad_normed.astype(jnp.float32) * norm_gain
    grad = inverse * (
        scaled
        - jnp.mean(scaled, axis=-1, keepdims=True)
        - unit * jnp.mean(scaled * unit, axis=-1, keepdims=True)
    )
    return (grad_out.astype(jnp.float32) + grad).astype(jnp.bfloat16)


def body(tokens, norm_gain, w_query, w_key, w_value, w_output, grad_out):
    full_query, full_key, full_value, full_output = (
        lax.all_gather(w_query, ("frame", "space"), axis=0, tiled=True),
        lax.all_gather(w_key, ("frame", "space"), axis=0, tiled=True),
        lax.all_gather(w_value, ("frame", "space"), axis=0, tiled=True),
        lax.all_gather(w_output, ("frame", "space"), axis=0, tiled=True),
    )
    normed, unit, inverse = normalize(tokens, norm_gain)
    normed_pixels, grad_pixels = (
        lax.all_to_all(normed, "frame", split_axis=1, concat_axis=0, tiled=True),
        lax.all_to_all(grad_out, "frame", split_axis=1, concat_axis=0, tiled=True),
    )
    query_heads = split_heads(project(normed_pixels, full_query).astype(jnp.bfloat16))
    key_heads = split_heads(project(normed_pixels, full_key).astype(jnp.bfloat16))
    value_heads = split_heads(project(normed_pixels, full_value).astype(jnp.bfloat16))
    grad_heads = split_heads(project_back(grad_pixels, full_output).astype(jnp.bfloat16))
    grad_query, grad_key, grad_value = attend_back(query_heads, key_heads, value_heads, grad_heads)
    normed_grad_pixels = (
        project_back(join_heads(grad_query), full_query)
        + project_back(join_heads(grad_key), full_key)
        + project_back(join_heads(grad_value), full_value)
    ).astype(jnp.bfloat16)
    grad_normed = lax.all_to_all(
        normed_grad_pixels, "frame", split_axis=0, concat_axis=1, tiled=True
    )
    return norm_back(grad_out, grad_normed, unit, inverse, norm_gain)


def solution(mesh):
    placed = (
        P(("groups", "frame"), "space", None),
        P(),
        P(("frame", "space"), None),
        P(("frame", "space"), None),
        P(("frame", "space"), None),
        P(("frame", "space"), None),
        P(("groups", "frame"), "space", None),
    )
    return jax.shard_map(
        body,
        mesh=mesh,
        in_specs=placed,
        out_specs=P(("groups", "frame"), "space", None),
        check_vma=False,
    )
```

profile of v0, /device:TPU:0, one launch (start us, length us, event | category | flops | bytes accessed | tf_op | source)
XLA Modules:
  0.0 237.7 jit_solution(16953589642717350258)
XLA Ops:
  9.3 2.4 copy.75
  11.7 4.2 %all-to-all-start.1 = ((bf16[2,128,1024]{2,0,1:T(2,128)(2,1)}), bf16[2,128,1024]{2,0,1:T(2,128)(2,1)S(1)}, u32[]{:S(2)}, u32[]{:S(2)}) async-start(bf16[2,128,1024]{2,0,1:T(2,128)(2,1)} %copy.75), calls=%async_computation.1 | async-start | bytes 1048576 | tf_op jit(solution)/shard_map/all_to_all | solution.py:89
  16.7 1.4 copy.71
  18.1 8.1 %all-to-all-done.1 = bf16[2,128,1024]{2,0,1:T(2,128)(2,1)S(1)} async-done(((bf16[2,128,1024]{2,0,1:T(2,128)(2,1)}), bf16[2,128,1024]{2,0,1:T(2,128)(2,1)S(1)}, u32[]{:S(2)}, u32[]{:S(2)}) %all-to-all-start.1) | async-done | bytes 524320 | tf_op jit(solution)/shard_map/all_to_all | solution.py:89
  26.2 3.6 %all-to-all-start = ((bf16[2,128,1024]{2,0,1:T(2,128)(2,1)}), bf16[2,128,1024]{2,0,1:T(2,128)(2,1)S(1)}, u32[]{:S(2)}, u32[]{:S(2)}) async-start(bf16[2,128,1024]{2,0,1:T(2,128)(2,1)} %copy.71), calls=%async_computation | async-start | bytes 1048576 | tf_op jit(solution)/shard_map/all_to_all | solution.py:88
  29.9 8.5 %all-to-all-done = bf16[2,128,1024]{2,0,1:T(2,128)(2,1)S(1)} async-done(((bf16[2,128,1024]{2,0,1:T(2,128)(2,1)}), bf16[2,128,1024]{2,0,1:T(2,128)(2,1)S(1)}, u32[]{:S(2)}, u32[]{:S(2)}) %all-to-all-start) | async-done | bytes 524320 | tf_op jit(solution)/shard_map/all_to_all | solution.py:88
  38.6 16.3 %all-gather.9.cloned.1.call-done = bf16[1024,1024]{1,0:T(8,128)(2,1)} async-done(((bf16[64,1024]{1,0:T(8,128)(2,1)}), bf16[1024,1024]{1,0:T(8,128)(2,1)}) %all-gather.9.cloned.1.call-update) | async-done | bytes 2097168 | tf_op jit(solution)/shard_map/all_gather | solution.py:84
  54.9 2.3 fusion.38
  57.9 39.4 %all-gather.5.cloned.1.call-done = bf16[1024,1024]{1,0:T(8,128)(2,1)} async-done(((bf16[64,1024]{1,0:T(8,128)(2,1)}), bf16[1024,1024]{1,0:T(8,128)(2,1)}) %all-gather.5.cloned.1.call-update) | async-done | bytes 2097168 | tf_op jit(solution)/shard_map/all_gather | solution.py:82
  97.2 2.3 fusion.32
  99.6 1.6 reshape.75
  101.2 38.4 %all-gather.7.cloned.1.call-done = bf16[1024,1024]{1,0:T(8,128)(2,1)} async-done(((bf16[64,1024]{1,0:T(8,128)(2,1)}), bf16[1024,1024]{1,0:T(8,128)(2,1)}) %all-gather.7.cloned.1.call-update) | async-done | bytes 2097168 | tf_op jit(solution)/shard_map/all_gather | solution.py:81
  139.6 2.3 fusion.35
  141.9 1.6 reshape.76
  143.6 38.3 %all-gather.11.cloned.1.call-done = bf16[1024,1024]{1,0:T(8,128)(2,1)} async-done(((bf16[64,1024]{1,0:T(8,128)(2,1)}), bf16[1024,1024]{1,0:T(8,128)(2,1)}) %all-gather.11.cloned.1.call-update) | async-done | bytes 2097168 | tf_op jit(solution)/shard_map/all_gather | solution.py:83
  181.8 2.3 fusion.41
  184.8 5.0 %fusion.89 = (f32[32,16,8]{2,1,0:T(8,128)S(1)}, f32[32,16,8,8]{2,3,1,0:T(8,128)}) fusion(bf16[8,32,16,64]{3,2,1,0:T(8,128)(2,1)} %reshape.75, bf16[8,32,16,64]{3,2,1,0:T(8,128)(2,1)} %reshape.76), kind=kOutput, calls=%fused_computation.74 | convolution fusion | flops 4292615 | bytes 1196032 | tf_op jit(solution)/shard_map/sub | solution.py:48
  189.8 2.7 %fusion.57 = f32[32,16,8,8]{2,3,1,0:T(8,128)} fusion(bf16[8,32,16,64]{3,2,1,0:T(8,128)(2,1)S(1)} %reshape.78, bf16[8,32,16,64]{3,2,1,0:T(8,128)(2,1)S(1)} %reshape.77), kind=kOutput, calls=%fused_computation.53 | convolution fusion | flops 4194304 | bytes 1179648 | tf_op jit(solution)/shard_map/fphd,gphd->phfg/dot_general | solution.py:55
  192.5 2.0 fusion.22
  194.5 6.5 %fusion.20 = bf16[8,32,16,64]{3,0,2,1:T(8,128)(2,1)} fusion(f32[32,16,8,8]{2,3,1,0:T(8,128)} %fusion.57, bf16[8,32,16,64]{3,2,1,0:T(8,128)(2,1)} %reshape.75, f32[32,16,8,8]{2,3,1,0:T(8,128)} %get-tuple-element.6, f32[32,16,8]{2,1,0:T(8,128)S(1)} %get-tuple-element.5), kind=kOutput, calls=%fused_computation.25 | convolution fusion | flops 4689927 | bytes 1327104 | tf_op jit(solution)/shard_map/phfg,gphd->fphd/dot_general | solution.py:60
  201.0 5.4 %fusion.21 = bf16[8,32,16,64]{3,0,2,1:T(8,128)(2,1)} fusion(f32[32,16,8,8]{2,3,1,0:T(8,128)S(1)} %copy-done.4, bf16[8,32,16,64]{3,2,1,0:T(8,128)(2,1)} %reshape.76, f32[32,16,8,8]{2,3,1,0:T(8,128)} %get-tuple-element.6, f32[32,16,8]{2,1,0:T(8,128)S(1)} %get-tuple-element.5), kind=kOutput, calls=%fused_computation.26 | convolution fusion | flops 4689927 | bytes 1327104 | tf_op jit(solution)/shard_map/phfg,fphd->gphd/dot_general | solution.py:63
  206.4 1.4 copy.85
  207.8 0.7 dot_general.61
  208.5 1.4 copy.81
  209.8 0.7 dot_general.55
  210.6 1.4 copy.83
  212.7 2.5 %fusion.2 = f32[8,32,1024]{2,1,0:T(8,128)S(1)} fusion(bf16[8,32,1024]{2,1,0:T(8,128)(2,1)S(1)} %dot_general.61, bf16[1024,1024]{1,0:T(8,128)(2,1)} %all-gather.11.cloned.1.call-done), kind=kOutput, calls=%fused_computation.2 | convolution fusion | flops 536870912 | bytes 3670016 | tf_op jit(solution)/shard_map/dot_general | solution.py:28
  215.2 0.7 fusion.8
  215.9 0.8 copy-done.3
  216.7 0.8 fusion.29
  217.5 11.2 %all_to_all.39 = bf16[8,32,1024]{2,1,0:T(8,128)(2,1)S(1)} all-to-all(bf16[8,32,1024]{2,1,0:T(8,128)(2,1)S(1)} %fusion.29), channel_id=1, replica_groups=mesh['groups'=2,'frame'=4,'space'=4] {'frame'}, dimensions={0} | all-to-all | bytes 1048576 | tf_op jit(solution)/shard_map/all_to_all | solution.py:101
  229.9 1.2 fusion.54
  (39 shorter events, 6.9 us)
Async XLA Ops:
  6.5 9.4 %copy-start = (bf16[2,128,1024]{2,1,0:T(8,128)(2,1)S(1)}, bf16[2,128,1024]{2,1,0:T(8,128)(2,1)}, u32[]{:S(2)}) copy-start(bf16[2,128,1024]{2,1,0:T(8,128)(2,1)} %param.7) | copy-start | bytes 1572868
  6.5 9.8 %copy-start.5 = (f32[1024]{0:T(1024)S(1)}, f32[1024]{0:T(1024)}, u32[]{:S(2)}) copy-start(f32[1024]{0:T(1024)} %param.8) | copy-start | bytes 12292
  6.5 48.4 %all-gather.9.cloned.1.call-start = ((), (), s32[]{:S(2)}) async-start(), calls=%async_computation.5 | async-start | bytes 2228224 | tf_op jit(solution)/shard_map/all_gather | solution.py:84
  7.3 90.0 %all-gather.5.cloned.1.call-start = ((), (), s32[]{:S(2)}) async-start(), calls=%async_computation.3 | async-start | bytes 2228224 | tf_op jit(solution)/shard_map/all_gather | solution.py:82
  8.0 131.6 %all-gather.7.cloned.1.call-start = ((), (), s32[]{:S(2)}) async-start(), calls=%async_computation.4 | async-start | bytes 2228224 | tf_op jit(solution)/shard_map/all_gather | solution.py:81
  8.7 173.1 %all-gather.11.cloned.1.call-start = ((), (), s32[]{:S(2)}) async-start(), calls=%async_computation.6 | async-start | bytes 2228224 | tf_op jit(solution)/shard_map/all_gather | solution.py:83
  11.7 14.5 %all-to-all-start.1 = ((bf16[2,128,1024]{2,0,1:T(2,128)(2,1)}), bf16[2,128,1024]{2,0,1:T(2,128)(2,1)S(1)}, u32[]{:S(2)}, u32[]{:S(2)}) async-start(bf16[2,128,1024]{2,0,1:T(2,128)(2,1)} %copy.75), calls=%async_computation.1 | async-start | bytes 1048576 | tf_op jit(solution)/shard_map/all_to_all | solution.py:89
  26.2 12.3 %all-to-all-start = ((bf16[2,128,1024]{2,0,1:T(2,128)(2,1)}), bf16[2,128,1024]{2,0,1:T(2,128)(2,1)S(1)}, u32[]{:S(2)}, u32[]{:S(2)}) async-start(bf16[2,128,1024]{2,0,1:T(2,128)(2,1)} %copy.71), calls=%async_computation | async-start | bytes 1048576 | tf_op jit(solution)/shard_map/all_to_all | solution.py:88
  189.8 2.7 %copy-start.6 = (f32[32,16,8,8]{2,3,1,0:T(8,128)S(1)}, f32[32,16,8,8]{2,3,1,0:T(8,128)}, u32[]{:S(2)}) copy-start(f32[32,16,8,8]{2,3,1,0:T(8,128)} %get-tuple-element.6) | copy-start | bytes 393220
  194.5 6.5 %copy-start.4 = (f32[32,16,8,8]{2,3,1,0:T(8,128)S(1)}, f32[32,16,8,8]{2,3,1,0:T(8,128)}, u32[]{:S(2)}) copy-start(f32[32,16,8,8]{2,3,1,0:T(8,128)} %fusion.57) | copy-start | bytes 393220
  212.6 2.5 %copy-start.1 = (bf16[1024,1024]{1,0:T(8,128)(2,1)S(1)}, bf16[1024,1024]{1,0:T(8,128)(2,1)}, u32[]{:S(2)}) copy-start(bf16[1024,1024]{1,0:T(8,128)(2,1)} %all-gather.7.cloned.1.call-done) | copy-start | bytes 6291460
  215.2 1.6 copy-start.3
  228.9 1.0 copy-start.2
Sparse Core Ops, SparseCore 0:
  9.6 45.2 all-gather.8
  57.1 40.0 all-gather.4
  99.5 40.0 all-gather.6
  141.7 40.0 all-gather.10
where the time goes:
time: 238 us
  waiting for transfers between devices  152 us (64%)
  matrix products  34.8 us (15%)
  local copies, waits for them, and re-layouts  16.1 us (7%)
  between operations  13.3 us (6%)
  blocking collectives  11.2 us (5%)
  starting transfers between devices  7.97 us (3%)
  other arithmetic  2.63 us (1%)
    all_gather x1, waiting for transfers between devices, body(): lax.all_gather(w_key, ('frame', 'space'), axis=0, tiled=True)  39.4 us
    all_gather x1, waiting for transfers between devices, body(): lax.all_gather(w_query, ('frame', 'space'), axis=0, tiled=True)  38.4 us
    all_gather x1, waiting for transfers between devices, body(): lax.all_gather(w_value, ('frame', 'space'), axis=0, tiled=True)  38.3 us
    all_gather x1, waiting for transfers between devices, body(): lax.all_gather(w_output, ('frame', 'space'), axis=0, tiled=True)  16.3 us
    all_to_all x1, blocking collectives, body(): lax.all_to_all(normed_grad_pixels, 'frame', split_axis=0, concat_axis=1,...  11.2 us
    all_to_all x1, waiting for transfers between devices, body(): lax.all_to_all(normed, 'frame', split_axis=1, concat_axis=0, tiled=True)  8.51 us
    all_to_all x1, waiting for transfers between devices, body(): lax.all_to_all(grad_out, 'frame', split_axis=1, concat_axis=0, tiled=True)  8.1 us
    dot_general x3, matrix products, project(): result = jnp.dot(flat, weight, preferred_element_type=jnp.float32)  6.89 us
  transfers between devices with their start and end apart: 6, of which 6 were waited for; matrix products, arithmetic and copies ran while one was open for 7% of the time, Pallas kernels for 0%

commit v1 on v0

--- a/solution.py
+++ b/solution.py
@@ -1,6 +1,8 @@
 import jax
 import jax.numpy as jnp
 from jax import lax
+from jax.experimental import pallas as pl
+from jax.experimental.pallas import tpu as pltpu
 from jax.sharding import PartitionSpec as P
 
 HEADS = 16
@@ -104,6 +106,321 @@
     return norm_back(grad_out, grad_normed, unit, inverse, norm_gain)
 
 
+MESH = pl.DeviceIdType.MESH
+NT = (((1,), (1,)), ((), ()))
+TN = (((0,), (0,)), ((), ()))
+F32 = jnp.float32
+BF16 = jnp.bfloat16
+
+
+def kernel(
+    tok, gain, wo, wq, wk, wv, gout, out,
+    W, XG, XN, NS, U, INV, QQ, KK, VV, GA, DQ, DK, DV, PS, PO, SIBP, RS, RR,
+    loc, snd, rw, rs, ra, rb,
+):
+    g = lax.axis_index("groups")
+    f = lax.axis_index("frame")
+    z = lax.axis_index("space")
+    x = f // 2
+    c = f % 2
+    sib = (g, 2 * x + (1 - c), z)
+    xpeer = (g, 2 * (1 - x) + c, z)
+    ypeer = (1 - g, f, z)
+
+    def zdev(dz):
+        return (g, f, lax.rem(z + dz, 4))
+
+    weights = (wo, wq, wk, wv)
+    sends = []
+
+    def send(src, dst, rsem, dev):
+        d = pltpu.make_async_remote_copy(
+            src_ref=src, dst_ref=dst, send_sem=snd.at[len(sends)], recv_sem=rsem,
+            device_id=dev, device_id_type=MESH,
+        )
+        d.start()
+        sends.append(d)
+
+    def got(dst, rsem):
+        pltpu.make_async_remote_copy(
+            src_ref=dst, dst_ref=dst, send_sem=snd.at[0], recv_sem=rsem,
+            device_id=sib, device_id_type=MESH,
+        ).wait_recv()
+
+    locs = []
+
+    def local(src, dst):
+        d = pltpu.make_async_copy(src, dst, loc.at[len(locs)])
+        d.start()
+        locs.append(d)
+
+    for e in range(2):
+        local(wo.at[:, pl.ds(512 * e, 512)], W.at[0, x, e, z])
+    for m in range(1, 4):
+        for half in range(2):
+            col = pl.multiple_of(512 * half + 256 * c, 256)
+            local(weights[m].at[:, pl.ds(col, 256)], W.at[m, x, c, z, :, pl.ds(256 * half, 256)])
+
+    barrier = pltpu.get_barrier_semaphore()
+    peers = (sib, xpeer, ypeer, zdev(1), zdev(2), zdev(3))
+    for p in peers:
+        pl.semaphore_signal(barrier, inc=1, device_id=p, device_id_type=MESH)
+    pl.semaphore_wait(barrier, len(peers))
+
+    for m in range(1, 4):
+        for half in range(2):
+            col = pl.multiple_of(512 * half + 256 * (1 - c), 256)
+            send(
+                weights[m].at[:, pl.ds(col, 256)],
+                W.at[m, x, c, z, :, pl.ds(256 * half, 256)],
+                rs.at[m - 1, half], sib,
+            )
+    for fr in range(2):
+        send(gout.at[fr, 1 - x], XG.at[:, 2, fr], ra.at[0, 1, fr], xpeer)
+        send(gout.at[fr, x], XG.at[:, 1, fr], ra.at[0, 0, fr], sib)
+        XG[:, 0, fr] = gout[fr, x]
+
+    for d in locs:
+        d.wait()
+    for m in range(1, 4):
+        for half in range(2):
+            got(W.at[m, x, 1 - c, z, :, pl.ds(256 * half, 256)], rs.at[m - 1, half])
+
+    def unit_at(m, xi, zi):
+        return W.at[m, xi, :, zi]
+
+    def send_unit(m, xi, zi, dev):
+        send(unit_at(m, xi, zi), unit_at(m, xi, zi), rw.at[m, xi, zi], dev)
+
+    def got_unit(m, xi, zi):
+        got(unit_at(m, xi, zi), rw.at[m, xi, zi])
+
+    m0 = g
+    m0o = 1 - g
+    m1 = 2 + g
+    m1o = 3 - g
+    for dz in (1, 2, 3):
+        send_unit(m0, x, z, zdev(dz))
+
+    gains = gain[...]
+
+    def norm(half, fr):
+        values = tok[fr, half].astype(F32).reshape(64, 1024)
+        centred = values - jnp.mean(values, axis=-1, keepdims=True)
+        inverse = lax.rsqrt(jnp.mean(centred * centred, axis=-1, keepdims=True) + norm_epsilon)
+        unit = centred * inverse
+        U[fr, half] = unit.reshape(4, 16, 1024)
+        INV[fr, half] = jnp.broadcast_to(inverse, (64, 128)).reshape(4, 16, 128)
+        return (unit * gains).astype(BF16).reshape(4, 16, 1024)
+
+    for fr in range(2):
+        NS[:, fr] = norm(1 - x, fr)
+    send(NS, XN.at[:, 2], ra.at[1, 1, 0], xpeer)
+    send_unit(m0, x, z, xpeer)
+    for dz in (1, 2, 3):
+        send_unit(m1, x, z, zdev(dz))
+    send_unit(m1, x, z, xpeer)
+    for dz in (1, 2, 3):
+        send_unit(m1o, x, z, zdev(dz))
+    for fr in range(2):
+        XN[:, 0, fr] = norm(x, fr)
+    send(XN.at[:, 0], XN.at[:, 1], ra.at[1, 0, 0], sib)
+
+    for fr in range(2):
+        got(XG.at[:, 2, fr], ra.at[0, 1, fr])
+    send(XG.at[:, 2], XG.at[:, 3], rb.at[0], sib)
+    got(XN.at[:, 2], ra.at[1, 1, 0])
+    send(XN.at[:, 2], XN.at[:, 3], rb.at[1], sib)
+
+    for dz in (1, 3, 2):
+        zs = lax.rem(z + dz, 4)
+        got_unit(m0, x, zs)
+        send_unit(m0, x, zs, xpeer)
+        send_unit(m0, x, zs, ypeer)
+    for dz in (0, 1, 3, 2):
+        zs = lax.rem(z + dz, 4)
+        got_unit(m0, 1 - x, zs)
+        send_unit(m0, 1 - x, zs, ypeer)
+    for dz in (1, 3, 2):
+        zs = lax.rem(z + dz, 4)
+        got_unit(m1, x, zs)
+        send_unit(m1, x, zs, xpeer)
+
+    for fr in range(2):
+        got(XG.at[:, 1, fr], ra.at[0, 0, fr])
+    got(XN.at[:, 1], ra.at[1, 0, 0])
+    got(XG.at[:, 3], rb.at[0])
+    got(XN.at[:, 3], rb.at[1])
+
+    for dz in (1, 3, 2):
+        got_unit(m0o, x, lax.rem(z + dz, 4))
+    for dz in (0, 1, 3, 2):
+        got_unit(m0o, 1 - x, lax.rem(z + dz, 4))
+
+    def weight(m):
+        return W[m].reshape(1024, 512)
+
+    def project_in(m, dst):
+        dst[...] = jnp.dot(
+            XN[...].reshape(512, 1024), weight(m), preferred_element_type=F32
+        ).astype(BF16)
+
+    grad = XG[...].reshape(512, 1024)
+    GA[...] = (
+        lax.dot_general(grad[:, :512], W[0, :, 0].reshape(512, 512), NT, preferred_element_type=F32)
+        + lax.dot_general(grad[:, 512:], W[0, :, 1].reshape(512, 512), NT, preferred_element_type=F32)
+    ).astype(BF16)
+
+    for dz in (0, 1, 3, 2):
+        zs = lax.rem(z + dz, 4)
+        got_unit(m1, 1 - x, zs)
+        send_unit(m1, 1 - x, zs, ypeer)
+
+    project_in(1, QQ)
+
+    for dz in (1, 3, 2):
+        got_unit(m1o, x, lax.rem(z + dz, 4))
+    for dz in (0, 1, 3, 2):
+        got_unit(m1o, 1 - x, lax.rem(z + dz, 4))
+    project_in(2, KK)
+    project_in(3, VV)
+
+    row = lax.broadcasted_iota(jnp.int32, (128, 256), 0)
+    lane = lax.broadcasted_iota(jnp.int32, (128, 256), 1)
+    same = (row & 15) == (lane & 15)
+    low = lax.broadcasted_iota(jnp.int32, (128, 128), 1) < 64
+    scaling = 0.125
+
+    def halves(a, fn):
+        left, right = fn(a[:, :128]), fn(a[:, 128:])
+        return jnp.concatenate(
+            [jnp.broadcast_to(left, (128, 128)), jnp.broadcast_to(right, (128, 128))], axis=1
+        )
+
+    def row_sum(a):
+        return jnp.sum(a, axis=-1, keepdims=True)
+
+    def row_max(a):
+        return jnp.max(a, axis=-1, keepdims=True)
+
+    def attend(tb, carry):
+        rows = pl.ds(pl.multiple_of(tb * 128, 128), 128)
+        for pair in range(4):
+            cols = pl.ds(128 * pair, 128)
+            q, k, v, go = QQ[rows, cols], KK[rows, cols], VV[rows, cols], GA[rows, cols]
+            zero = jnp.zeros_like(k)
+            k2 = jnp.concatenate([jnp.where(low, k, zero), jnp.where(low, zero, k)], axis=0)
+            v2 = jnp.concatenate([jnp.where(low, v, zero), jnp.where(low, zero, v)], axis=0)
+            s = lax.dot_general(q, k2, NT, preferred_element_type=F32) * scaling
+            s = jnp.where(same, s, -1e30)
+            ex = jnp.exp(s - halves(s, row_max))
+            prob = ex * (1.0 / halves(ex, row_sum))
+            low_p = prob.astype(BF16)
+            gp = lax.dot_general(go, v2, NT, preferred_element_type=F32)
+            ds = (prob * (gp - halves(prob * gp, row_sum)) * scaling).astype(BF16)
+            DQ[rows, cols] = jnp.dot(ds, k2, preferred_element_type=F32).astype(BF16)
+            dk = lax.dot_general(ds, q, TN, preferred_element_type=F32)
+            DK[rows, cols] = jnp.where(low, dk[:128], dk[128:]).astype(BF16)
+            dv = lax.dot_general(low_p, go, TN, preferred_element_type=F32)
+            DV[rows, cols] = jnp.where(low, dv[:128], dv[128:]).astype(BF16)
+        return carry
+
+    def back(ch):
+        rows = pl.ds(256 * ch, 256)
+        part = (
+            lax.dot_general(DQ[rows], weight(1), NT, preferred_element_type=F32)
+            + lax.dot_general(DK[rows], weight(2), NT, preferred_element_type=F32)
+            + lax.dot_general(DV[rows], weight(3), NT, preferred_element_type=F32)
+        ).reshape(2, 4, 2, 16, 1024)
+        PS[ch, :, 0] = part[:, 1]
+        PS[ch, :, 1] = part[:, 3]
+        send(PS.at[ch], SIBP.at[ch], rb.at[2 + ch], sib)
+        PO[ch, :, 0] = part[:, 0]
+        PO[ch, :, 1] = part[:, 2]
+
+    def finish(ch, fr, half, grad_normed):
+        scaled = grad_normed.astype(F32).reshape(32, 1024) * gains
+        span = pl.ds(2 * ch, 2)
+        unit = U[fr, half, span].reshape(32, 1024)
+        inverse = INV[fr, half, span].reshape(32, 128)[:, :1]
+        grad_in = inverse * (
+            scaled
+            - jnp.mean(scaled, axis=-1, keepdims=True)
+            - unit * jnp.mean(scaled * unit, axis=-1, keepdims=True)
+        )
+        base = gout[fr, half, span].astype(F32).reshape(32, 1024)
+        out[fr, half, span] = (base + grad_in).astype(BF16).reshape(2, 16, 1024)
+
+    def combine(ch):
+        got(SIBP.at[ch], rb.at[2 + ch])
+        RS[ch] = (PO[ch, :, 1] + SIBP[ch, :, 1]).astype(BF16)
+        send(RS.at[ch], RR.at[ch], rb.at[4 + ch], xpeer)
+
+    def finish_own(ch):
+        for fr in range(2):
+            finish(ch, fr, x, (PO[ch, :, 0, fr] + SIBP[ch, :, 0, fr]).astype(BF16))
+
+    def finish_peer(ch):
+        got(RR.at[ch], rb.at[4 + ch])
+        for fr in range(2):
+            finish(ch, fr, 1 - x, RR[ch, :, fr])
+
+    lax.fori_loop(0, 2, attend, 0)
+    back(0)
+    lax.fori_loop(2, 4, attend, 0)
+    combine(0)
+    back(1)
+    finish_own(0)
+    combine(1)
+    finish_own(1)
+    finish_peer(0)
+    finish_peer(1)
+
+    for d in sends:
+        d.wait_send()
+
+
+def fused(tokens, norm_gain, w_query, w_key, w_value, w_output, grad_out):
+    shape = tokens.shape
+    cut = (2, 2, 4, 16, 1024)
+    vmem = pl.BlockSpec(memory_space=pltpu.VMEM)
+    anywhere = pl.BlockSpec(memory_space=pl.ANY)
+    act = (4, 4, 2, 16, 1024)
+    scratch = [
+        pltpu.VMEM((4, 2, 2, 4, 64, 512), BF16),
+        pltpu.VMEM(act, BF16),
+        pltpu.VMEM(act, BF16),
+        pltpu.VMEM((4, 2, 16, 1024), BF16),
+        pltpu.VMEM(cut, F32),
+        pltpu.VMEM((2, 2, 4, 16, 128), F32),
+    ]
+    scratch += [pltpu.VMEM((512, 512), BF16)] * 7
+    scratch += [pltpu.VMEM((2, 2, 2, 2, 16, 1024), F32)] * 3
+    scratch += [pltpu.VMEM((2, 2, 2, 16, 1024), BF16)] * 2
+    scratch += [
+        pltpu.SemaphoreType.DMA((8,)),
+        pltpu.SemaphoreType.DMA((64,)),
+        pltpu.SemaphoreType.DMA((4, 2, 4)),
+        pltpu.SemaphoreType.DMA((3, 2)),
+        pltpu.SemaphoreType.DMA((2, 2, 2)),
+        pltpu.SemaphoreType.DMA((6,)),
+    ]
+    result = pl.pallas_call(
+        kernel,
+        out_shape=jax.ShapeDtypeStruct(cut, BF16),
+        in_specs=[vmem, vmem, anywhere, anywhere, anywhere, anywhere, vmem],
+        out_specs=vmem,
+        scratch_shapes=scratch,
+        compiler_params=pltpu.CompilerParams(
+            collective_id=0, has_side_effects=True, vmem_limit_bytes=48 * 1024 * 1024
+        ),
+    )(
+        tokens.reshape(cut), norm_gain.reshape(1, 1024), w_output, w_query, w_key, w_value,
+        grad_out.reshape(cut),
+    )
+    return result.reshape(shape)
+
+
 def solution(mesh):
     placed = (
         P(("groups", "frame"), "space", None),
@@ -114,8 +431,9 @@
         P(("frame", "space"), None),
         P(("groups", "frame"), "space", None),
     )
+    sizes = tuple(mesh.shape[name] for name in ("groups", "frame", "space"))
     return jax.shard_map(
-        body,
+        fused if sizes == (2, 4, 4) else body,
         mesh=mesh,
         in_specs=placed,
         out_specs=P(("groups", "frame"), "space", None),

time: 238 us -> 84.8 us (0.36)
  the two profiles are of different devices: /device:TPU:0 before, /device:TPU:13 now
where the time goes in v1:
time: 84.8 us; the launch traced here: 84.5 us
  Pallas kernels  77.3 us (91%)
  local copies, waits for them, and re-layouts  7.18 us (8%)
    pallas_call x1, Pallas kernels, fused(): pl.pallas_call(kernel, out_shape=jax.ShapeDtypeStruct(cut, BF16), in_spec...  77.3 us
    unnamed x15, local copies, waits for them, and re-layouts  7.18 us

profile of v1, /device:TPU:13, one launch (start us, length us, event | category | flops | bytes accessed | tf_op | source)
XLA Modules:
  0.0 84.5 jit_solution(11916418320757008042)
XLA Ops:
  0.0 0.0 copy-start.6
  0.0 0.7 copy-done.6
  0.7 0.0 copy-start
  0.7 1.0 %copy-done = bf16[2,128,1024]{2,1,0:T(8,128)(2,1)S(1)} copy-done((bf16[2,128,1024]{2,1,0:T(8,128)(2,1)S(1)}, bf16[2,128,1024]{2,1,0:T(8,128)(2,1)}, u32[]{:S(2)}) %copy-start) | copy-done | bytes 524312
  1.7 0.0 copy-start.1
  1.7 1.0 %copy-done.1 = bf16[2,128,1024]{2,1,0:T(8,128)(2,1)S(1)} copy-done((bf16[2,128,1024]{2,1,0:T(8,128)(2,1)S(1)}, bf16[2,128,1024]{2,1,0:T(8,128)(2,1)}, u32[]{:S(2)}) %copy-start.1) | copy-done | bytes 524312
  2.8 0.0 copy-start.2
  2.8 0.9 %copy-done.2 = bf16[64,1024]{1,0:T(8,128)(2,1)S(1)} copy-done((bf16[64,1024]{1,0:T(8,128)(2,1)S(1)}, bf16[64,1024]{1,0:T(8,128)(2,1)}, u32[]{:S(2)}) %copy-start.2) | copy-done | bytes 131096
  3.7 0.0 copy-start.3
  3.7 0.9 %copy-done.3 = bf16[64,1024]{1,0:T(8,128)(2,1)S(1)} copy-done((bf16[64,1024]{1,0:T(8,128)(2,1)S(1)}, bf16[64,1024]{1,0:T(8,128)(2,1)}, u32[]{:S(2)}) %copy-start.3) | copy-done | bytes 131096
  4.6 0.0 copy-start.4
  4.6 0.9 %copy-done.4 = bf16[64,1024]{1,0:T(8,128)(2,1)S(1)} copy-done((bf16[64,1024]{1,0:T(8,128)(2,1)S(1)}, bf16[64,1024]{1,0:T(8,128)(2,1)}, u32[]{:S(2)}) %copy-start.4) | copy-done | bytes 131096
  5.5 0.0 copy-start.5
  5.5 0.9 %copy-done.5 = bf16[64,1024]{1,0:T(8,128)(2,1)S(1)} copy-done((bf16[64,1024]{1,0:T(8,128)(2,1)S(1)}, bf16[64,1024]{1,0:T(8,128)(2,1)}, u32[]{:S(2)}) %copy-start.5) | copy-done | bytes 131096
  6.4 77.3 %shard_map.73 = bf16[2,2,4,16,1024]{4,3,2,1,0:T(8,128)(2,1)S(1)} custom-call(bf16[2,2,4,16,1024]{4,3,2,1,0:T(8,128)(2,1)S(1)} %bitcast.5, f32[1,1024]{1,0:T(1,128)S(1)} %bitcast.7, bf16[64,1024]{1,0:T(8,128)(2,1)S(1)} %copy-done.2, bf16[64,1024]{1,0:T(8,128)(2,1)S(1)} %copy-done.3, bf16[64,1024]{1,0:T(8,128)(2,1)S(1)} %copy-done.4, ...), custom_call_target="tpu_custom_call" | custom-call | tf_op jit(solution)/shard_map/pallas_call | solution.py:408
  83.7 0.8 copy.9
Async XLA Ops:
  0.0 0.7 copy-start.6
  0.7 1.0 %copy-start = (bf16[2,128,1024]{2,1,0:T(8,128)(2,1)S(1)}, bf16[2,128,1024]{2,1,0:T(8,128)(2,1)}, u32[]{:S(2)}) copy-start(bf16[2,128,1024]{2,1,0:T(8,128)(2,1)} %param.7) | copy-start | bytes 1572868
  1.7 1.0 %copy-start.1 = (bf16[2,128,1024]{2,1,0:T(8,128)(2,1)S(1)}, bf16[2,128,1024]{2,1,0:T(8,128)(2,1)}, u32[]{:S(2)}) copy-start(bf16[2,128,1024]{2,1,0:T(8,128)(2,1)} %param.13) | copy-start | bytes 1572868
  2.8 0.9 %copy-start.2 = (bf16[64,1024]{1,0:T(8,128)(2,1)S(1)}, bf16[64,1024]{1,0:T(8,128)(2,1)}, u32[]{:S(2)}) copy-start(bf16[64,1024]{1,0:T(8,128)(2,1)} %wo.1) | copy-start | bytes 393220
  3.7 0.9 %copy-start.3 = (bf16[64,1024]{1,0:T(8,128)(2,1)S(1)}, bf16[64,1024]{1,0:T(8,128)(2,1)}, u32[]{:S(2)}) copy-start(bf16[64,1024]{1,0:T(8,128)(2,1)} %wq.1) | copy-start | bytes 393220
  4.6 0.9 %copy-start.4 = (bf16[64,1024]{1,0:T(8,128)(2,1)S(1)}, bf16[64,1024]{1,0:T(8,128)(2,1)}, u32[]{:S(2)}) copy-start(bf16[64,1024]{1,0:T(8,128)(2,1)} %wk.1) | copy-start | bytes 393220
  5.5 0.9 %copy-start.5 = (bf16[64,1024]{1,0:T(8,128)(2,1)S(1)}, bf16[64,1024]{1,0:T(8,128)(2,1)}, u32[]{:S(2)}) copy-start(bf16[64,1024]{1,0:T(8,128)(2,1)} %wv.1) | copy-start | bytes 393220

commit v2 on v1

--- a/solution.py
+++ b/solution.py
@@ -1,3 +1,5 @@
+import functools
+
 import jax
 import jax.numpy as jnp
 from jax import lax
@@ -111,11 +113,12 @@
 TN = (((0,), (0,)), ((), ()))
 F32 = jnp.float32
 BF16 = jnp.bfloat16
+ZFULL = (False, True, True)
 
 
 def kernel(
-    tok, gain, wo, wq, wk, wv, gout, out,
-    W, XG, XN, NS, U, INV, QQ, KK, VV, GA, DQ, DK, DV, PS, PO, SIBP, RS, RR,
+    tok_in, gain, wo, wq, wk, wv, gout_in, out,
+    tok, gout, WO, WQ, XG, XN, NS, U, INV, QQ, KK, VV, DQ, DK, DV, GA, PA, PS, PO, SIBP, RS, RR,
     loc, snd, rw, rs, ra, rb,
 ):
     g = lax.axis_index("groups")
@@ -126,20 +129,24 @@
     sib = (g, 2 * x + (1 - c), z)
     xpeer = (g, 2 * (1 - x) + c, z)
     ypeer = (1 - g, f, z)
-
-    def zdev(dz):
-        return (g, f, lax.rem(z + dz, 4))
-
-    weights = (wo, wq, wk, wv)
+    up = (g, f, lax.rem(z + 1, 4))
+    down = (g, f, lax.rem(z + 3, 4))
+    has_up = z < 3
+    has_down = z > 0
+
+    weights = (wq, wk, wv)
     sends = []
 
-    def send(src, dst, rsem, dev):
+    def send(src, dst, rsem, dev, when=None):
         d = pltpu.make_async_remote_copy(
             src_ref=src, dst_ref=dst, send_sem=snd.at[len(sends)], recv_sem=rsem,
             device_id=dev, device_id_type=MESH,
         )
-        d.start()
-        sends.append(d)
+        sends.append((d, when))
+        if when is None:
+            d.start()
+        else:
+            pl.when(when)(d.start)
 
     def got(dst, rsem):
         pltpu.make_async_remote_copy(
@@ -155,52 +162,116 @@
         locs.append(d)
 
     for e in range(2):
-        local(wo.at[:, pl.ds(512 * e, 512)], W.at[0, x, e, z])
-    for m in range(1, 4):
+        local(wo.at[:, pl.ds(512 * e, 512)], WO.at[x, e, z])
+    local(tok_in, tok)
+    local(gout_in, gout)
+    for m in range(3):
         for half in range(2):
             col = pl.multiple_of(512 * half + 256 * c, 256)
-            local(weights[m].at[:, pl.ds(col, 256)], W.at[m, x, c, z, :, pl.ds(256 * half, 256)])
+            local(weights[m].at[:, pl.ds(col, 256)], WQ.at[half, m, x, c, z])
 
     barrier = pltpu.get_barrier_semaphore()
-    peers = (sib, xpeer, ypeer, zdev(1), zdev(2), zdev(3))
-    for p in peers:
+    for p in (sib, xpeer, ypeer):
         pl.semaphore_signal(barrier, inc=1, device_id=p, device_id_type=MESH)
-    pl.semaphore_wait(barrier, len(peers))
-
-    for m in range(1, 4):
+
+    @pl.when(has_up)
+    def _():
+        pl.semaphore_signal(barrier, inc=1, device_id=up, device_id_type=MESH)
+
+    @pl.when(has_down)
+    def _():
+        pl.semaphore_signal(barrier, inc=1, device_id=down, device_id_type=MESH)
+
+    pl.semaphore_wait(barrier, 3 + has_up.astype(jnp.int32) + has_down.astype(jnp.int32))
+
+    def piece(ph, xi, e, zi):
+        if ph == 0:
+            return WO.at[xi, e, zi]
+        return WQ.at[ph - 1, :, xi, e, zi]
+
+    def send_piece(ph, xi, e, zi, dev, when=None):
+        region = piece(ph, xi, e, zi)
+        send(region, region, rw.at[ph, xi, e, zi], dev, when)
+
+    def got_piece(ph, xi, e, zi):
+        got(piece(ph, xi, e, zi), rw.at[ph, xi, e, zi])
+
+    def planes(ph):
+        return (g, 1 - g) if ZFULL[ph] else (g,)
+
+    def own_z(ph):
+        for e in planes(ph):
+            send_piece(ph, x, e, z, up, has_up)
+            send_piece(ph, x, e, z, down, has_down)
+
+    def own_x(ph):
+        send_piece(ph, x, g, z, xpeer)
+
+    def relay_z(ph, d):
+        for below in (True, False):
+            here = (z >= d) if below else (z + d <= 3)
+            on = jnp.logical_and(here, has_up if below else has_down)
+            zi = lax.rem(z + (4 - d if below else d), 4)
+            for k, e in enumerate(planes(ph)):
+                @pl.when(here)
+                def _():
+                    got_piece(ph, x, e, zi)
+
+                send_piece(ph, x, e, zi, up if below else down, on)
+                if k == 0:
+                    send_piece(ph, x, e, zi, xpeer, here)
+                    if not ZFULL[ph]:
+                        send_piece(ph, x, e, zi, ypeer, here)
+
+    def relay_x(ph, d):
+        if d == 0:
+            got_piece(ph, 1 - x, g, z)
+            send_piece(ph, 1 - x, g, z, ypeer)
+            return
+        for below in (True, False):
+            here = (z >= d) if below else (z + d <= 3)
+            zi = lax.rem(z + (4 - d if below else d), 4)
+
+            @pl.when(here)
+            def _():
+                got_piece(ph, 1 - x, g, zi)
+
+            send_piece(ph, 1 - x, g, zi, ypeer, here)
+
+    def rest(ph):
+        if not ZFULL[ph]:
+            for dz in (1, 3, 2):
+                got_piece(ph, x, 1 - g, lax.rem(z + dz, 4))
+        for dz in (0, 1, 3, 2):
+            got_piece(ph, 1 - x, 1 - g, lax.rem(z + dz, 4))
+
+    def steps(ph):
+        return [
+            functools.partial(relay_z, ph, 1),
+            functools.partial(relay_x, ph, 0),
+            functools.partial(relay_z, ph, 2),
+            functools.partial(relay_x, ph, 1),
+            functools.partial(relay_z, ph, 3),
+            functools.partial(relay_x, ph, 2),
+            functools.partial(relay_x, ph, 3),
+        ]
+
+    for d in locs[:2]:
+        d.wait()
+    own_z(0)
+    own_x(0)
+    for fr in range(2):
+        send(gout_in.at[fr, 1 - x], XG.at[:, 2, fr], ra.at[0, 1, fr], xpeer)
+    for m in range(3):
         for half in range(2):
             col = pl.multiple_of(512 * half + 256 * (1 - c), 256)
             send(
-                weights[m].at[:, pl.ds(col, 256)],
-                W.at[m, x, c, z, :, pl.ds(256 * half, 256)],
-                rs.at[m - 1, half], sib,
+                weights[m].at[:, pl.ds(col, 256)], WQ.at[half, m, x, c, z], rs.at[m, half], sib
             )
     for fr in range(2):
-        send(gout.at[fr, 1 - x], XG.at[:, 2, fr], ra.at[0, 1, fr], xpeer)
-        send(gout.at[fr, x], XG.at[:, 1, fr], ra.at[0, 0, fr], sib)
-        XG[:, 0, fr] = gout[fr, x]
-
-    for d in locs:
+        send(gout_in.at[fr, x], XG.at[:, 1, fr], ra.at[0, 0, fr], sib)
+    for d in locs[2:]:
         d.wait()
-    for m in range(1, 4):
-        for half in range(2):
-            got(W.at[m, x, 1 - c, z, :, pl.ds(256 * half, 256)], rs.at[m - 1, half])
-
-    def unit_at(m, xi, zi):
-        return W.at[m, xi, :, zi]
-
-    def send_unit(m, xi, zi, dev):
-        send(unit_at(m, xi, zi), unit_at(m, xi, zi), rw.at[m, xi, zi], dev)
-
-    def got_unit(m, xi, zi):
-        got(unit_at(m, xi, zi), rw.at[m, xi, zi])
-
-    m0 = g
-    m0o = 1 - g
-    m1 = 2 + g
-    m1o = 3 - g
-    for dz in (1, 2, 3):
-        send_unit(m0, x, z, zdev(dz))
 
     gains = gain[...]
 
@@ -216,74 +287,48 @@
     for fr in range(2):
         NS[:, fr] = norm(1 - x, fr)
     send(NS, XN.at[:, 2], ra.at[1, 1, 0], xpeer)
-    send_unit(m0, x, z, xpeer)
-    for dz in (1, 2, 3):
-        send_unit(m1, x, z, zdev(dz))
-    send_unit(m1, x, z, xpeer)
-    for dz in (1, 2, 3):
-        send_unit(m1o, x, z, zdev(dz))
+    for m in range(3):
+        for half in range(2):
+            got(WQ.at[half, m, x, 1 - c, z], rs.at[m, half])
+    own_z(1)
+    own_x(1)
+    first = steps(0)
+    first[0]()
     for fr in range(2):
         XN[:, 0, fr] = norm(x, fr)
+        XG[:, 0, fr] = gout[fr, x]
     send(XN.at[:, 0], XN.at[:, 1], ra.at[1, 0, 0], sib)
-
+    for step in first[1:4]:
+        step()
     for fr in range(2):
         got(XG.at[:, 2, fr], ra.at[0, 1, fr])
     send(XG.at[:, 2], XG.at[:, 3], rb.at[0], sib)
+    for step in first[4:]:
+        step()
+    own_z(2)
+    own_x(2)
     got(XN.at[:, 2], ra.at[1, 1, 0])
     send(XN.at[:, 2], XN.at[:, 3], rb.at[1], sib)
-
-    for dz in (1, 3, 2):
-        zs = lax.rem(z + dz, 4)
-        got_unit(m0, x, zs)
-        send_unit(m0, x, zs, xpeer)
-        send_unit(m0, x, zs, ypeer)
-    for dz in (0, 1, 3, 2):
-        zs = lax.rem(z + dz, 4)
-        got_unit(m0, 1 - x, zs)
-        send_unit(m0, 1 - x, zs, ypeer)
-    for dz in (1, 3, 2):
-        zs = lax.rem(z + dz, 4)
-        got_unit(m1, x, zs)
-        send_unit(m1, x, zs, xpeer)
-
-    for fr in range(2):
-        got(XG.at[:, 1, fr], ra.at[0, 0, fr])
-    got(XN.at[:, 1], ra.at[1, 0, 0])
-    got(XG.at[:, 3], rb.at[0])
-    got(XN.at[:, 3], rb.at[1])
-
-    for dz in (1, 3, 2):
-        got_unit(m0o, x, lax.rem(z + dz, 4))
-    for dz in (0, 1, 3, 2):
-        got_unit(m0o, 1 - x, lax.rem(z + dz, 4))
-
-    def weight(m):
-        return W[m].reshape(1024, 512)
-
-    def project_in(m, dst):
-        dst[...] = jnp.dot(
-            XN[...].reshape(512, 1024), weight(m), preferred_element_type=F32
+    second = steps(1)
+    for step in second:
+        step()
+
+    def weight(half, m):
+        return WQ[half, m].reshape(1024, 256)
+
+    def project_in(half, m):
+        (QQ, KK, VV)[m][...] = jnp.dot(
+            XN[...].reshape(512, 1024), weight(half, m), preferred_element_type=F32
         ).astype(BF16)
 
-    grad = XG[...].reshape(512, 1024)
-    GA[...] = (
-        lax.dot_general(grad[:, :512], W[0, :, 0].reshape(512, 512), NT, preferred_element_type=F32)
-        + lax.dot_general(grad[:, 512:], W[0, :, 1].reshape(512, 512), NT, preferred_element_type=F32)
-    ).astype(BF16)
-
-    for dz in (0, 1, 3, 2):
-        zs = lax.rem(z + dz, 4)
-        got_unit(m1, 1 - x, zs)
-        send_unit(m1, 1 - x, zs, ypeer)
-
-    project_in(1, QQ)
-
-    for dz in (1, 3, 2):
-        got_unit(m1o, x, lax.rem(z + dz, 4))
-    for dz in (0, 1, 3, 2):
-        got_unit(m1o, 1 - x, lax.rem(z + dz, 4))
-    project_in(2, KK)
-    project_in(3, VV)
+    def project_grad(part):
+        span = pl.ds(2 * part, 2)
+        rows = pl.ds(256 * part, 256)
+        grad = XG[span].reshape(256, 1024)
+        GA[rows] = (
+            lax.dot_general(grad[:, :512], WO[:, 0].reshape(512, 512), NT, preferred_element_type=F32)
+            + lax.dot_general(grad[:, 512:], WO[:, 1].reshape(512, 512), NT, preferred_element_type=F32)
+        ).astype(BF16)
 
     row = lax.broadcasted_iota(jnp.int32, (128, 256), 0)
     lane = lax.broadcasted_iota(jnp.int32, (128, 256), 1)
@@ -303,11 +348,12 @@
     def row_max(a):
         return jnp.max(a, axis=-1, keepdims=True)
 
-    def attend(tb, carry):
+    def attend(half, tb, carry):
         rows = pl.ds(pl.multiple_of(tb * 128, 128), 128)
-        for pair in range(4):
+        for pair in range(2):
             cols = pl.ds(128 * pair, 128)
-            q, k, v, go = QQ[rows, cols], KK[rows, cols], VV[rows, cols], GA[rows, cols]
+            q, k, v = QQ[rows, cols], KK[rows, cols], VV[rows, cols]
+            go = GA[rows, pl.ds(256 * half + 128 * pair, 128)]
             zero = jnp.zeros_like(k)
             k2 = jnp.concatenate([jnp.where(low, k, zero), jnp.where(low, zero, k)], axis=0)
             v2 = jnp.concatenate([jnp.where(low, v, zero), jnp.where(low, zero, v)], axis=0)
@@ -325,13 +371,22 @@
             DV[rows, cols] = jnp.where(low, dv[:128], dv[128:]).astype(BF16)
         return carry
 
-    def back(ch):
+    def attention(half, ch):
+        lax.fori_loop(2 * ch, 2 * ch + 2, functools.partial(attend, half), 0)
+
+    def back(half, ch):
         rows = pl.ds(256 * ch, 256)
-        part = (
-            lax.dot_general(DQ[rows], weight(1), NT, preferred_element_type=F32)
-            + lax.dot_general(DK[rows], weight(2), NT, preferred_element_type=F32)
-            + lax.dot_general(DV[rows], weight(3), NT, preferred_element_type=F32)
-        ).reshape(2, 4, 2, 16, 1024)
+        return (
+            lax.dot_general(DQ[rows], weight(half, 0), NT, preferred_element_type=F32)
+            + lax.dot_general(DK[rows], weight(half, 1), NT, preferred_element_type=F32)
+            + lax.dot_general(DV[rows], weight(half, 2), NT, preferred_element_type=F32)
+        )
+
+    def back_first(ch):
+        PA[ch] = back(0, ch)
+
+    def back_last(ch):
+        part = (back(1, ch) + PA[ch]).reshape(2, 4, 2, 16, 1024)
         PS[ch, :, 0] = part[:, 1]
         PS[ch, :, 1] = part[:, 3]
         send(PS.at[ch], SIBP.at[ch], rb.at[2 + ch], sib)
@@ -365,19 +420,47 @@
         for fr in range(2):
             finish(ch, fr, 1 - x, RR[ch, :, fr])
 
-    lax.fori_loop(0, 2, attend, 0)
-    back(0)
-    lax.fori_loop(2, 4, attend, 0)
+    def gather_rest():
+        for fr in range(2):
+            got(XG.at[:, 1, fr], ra.at[0, 0, fr])
+        got(XN.at[:, 1], ra.at[1, 0, 0])
+        got(XG.at[:, 3], rb.at[0])
+        got(XN.at[:, 3], rb.at[1])
+        rest(0)
+
+    work = [
+        [gather_rest, functools.partial(project_grad, 0)],
+        [functools.partial(project_grad, 1)],
+        [functools.partial(rest, 1), functools.partial(project_in, 0, 0)],
+        [functools.partial(project_in, 0, 1)],
+        [functools.partial(project_in, 0, 2)],
+        [functools.partial(attention, 0, 0)],
+        [functools.partial(attention, 0, 1), functools.partial(back_first, 0),
+         functools.partial(back_first, 1)],
+    ]
+    for step, tasks in zip(steps(2), work):
+        step()
+        for task in tasks:
+            task()
+    rest(2)
+    for m in range(3):
+        project_in(1, m)
+    attention(1, 0)
+    back_last(0)
+    attention(1, 1)
     combine(0)
-    back(1)
+    back_last(1)
     finish_own(0)
     combine(1)
     finish_own(1)
     finish_peer(0)
     finish_peer(1)
 
-    for d in sends:
-        d.wait_send()
+    for d, when in sends:
+        if when is None:
+            d.wait_send()
+        else:
+            pl.when(when)(d.wait_send)
 
 
 def fused(tokens, norm_gain, w_query, w_key, w_value, w_output, grad_out):
@@ -387,20 +470,24 @@
     anywhere = pl.BlockSpec(memory_space=pl.ANY)
     act = (4, 4, 2, 16, 1024)
     scratch = [
-        pltpu.VMEM((4, 2, 2, 4, 64, 512), BF16),
+        pltpu.VMEM(cut, BF16),
+        pltpu.VMEM(cut, BF16),
+        pltpu.VMEM((2, 2, 4, 64, 512), BF16),
+        pltpu.VMEM((2, 3, 2, 2, 4, 64, 256), BF16),
         pltpu.VMEM(act, BF16),
         pltpu.VMEM(act, BF16),
         pltpu.VMEM((4, 2, 16, 1024), BF16),
         pltpu.VMEM(cut, F32),
         pltpu.VMEM((2, 2, 4, 16, 128), F32),
     ]
-    scratch += [pltpu.VMEM((512, 512), BF16)] * 7
+    scratch += [pltpu.VMEM((512, 256), BF16)] * 6
+    scratch += [pltpu.VMEM((512, 512), BF16), pltpu.VMEM((2, 256, 1024), F32)]
     scratch += [pltpu.VMEM((2, 2, 2, 2, 16, 1024), F32)] * 3
     scratch += [pltpu.VMEM((2, 2, 2, 16, 1024), BF16)] * 2
     scratch += [
-        pltpu.SemaphoreType.DMA((8,)),
-        pltpu.SemaphoreType.DMA((64,)),
-        pltpu.SemaphoreType.DMA((4, 2, 4)),
+        pltpu.SemaphoreType.DMA((10,)),
+        pltpu.SemaphoreType.DMA((128,)),
+        pltpu.SemaphoreType.DMA((3, 2, 2, 4)),
         pltpu.SemaphoreType.DMA((3, 2)),
         pltpu.SemaphoreType.DMA((2, 2, 2)),
         pltpu.SemaphoreType.DMA((6,)),
@@ -408,11 +495,11 @@
     result = pl.pallas_call(
         kernel,
         out_shape=jax.ShapeDtypeStruct(cut, BF16),
-        in_specs=[vmem, vmem, anywhere, anywhere, anywhere, anywhere, vmem],
+        in_specs=[anywhere, vmem, anywhere, anywhere, anywhere, anywhere, anywhere],
         out_specs=vmem,
         scratch_shapes=scratch,
         compiler_params=pltpu.CompilerParams(
-            collective_id=0, has_side_effects=True, vmem_limit_bytes=48 * 1024 * 1024
+            collective_id=0, has_side_effects=True, vmem_limit_bytes=60 * 1024 * 1024
         ),
     )(
         tokens.reshape(cut), norm_gain.reshape(1, 1024), w_output, w_query, w_key, w_value,

time: 84.8 us -> 73.1 us (0.86)
  the two profiles are of different devices: /device:TPU:13 before, /device:TPU:0 now
where the time goes in v2:
time: 73.1 us; the launch traced here: 72.9 us
  Pallas kernels  71 us (97%)
  local copies, waits for them, and re-layouts  1.87 us (3%)
    pallas_call x1, Pallas kernels, fused(): pl.pallas_call(kernel, out_shape=jax.ShapeDtypeStruct(cut, BF16), in_spec...  71 us
    unnamed x1, local copies, waits for them, and re-layouts  1.87 us

profile of v2, /device:TPU:0, one launch (start us, length us, event | category | flops | bytes accessed | tf_op | source)
XLA Modules:
  0.0 72.9 jit_solution(4348426450531887877)
XLA Ops:
  0.0 71.0 %shard_map.73 = bf16[2,2,4,16,1024]{4,3,2,1,0:T(8,128)(2,1)} custom-call(bf16[2,2,4,16,1024]{4,3,2,1,0:T(8,128)(2,1)} %bitcast.5, f32[1,1024]{1,0:T(1,128)} %bitcast.7, bf16[64,1024]{1,0:T(8,128)(2,1)} %wo.1, bf16[64,1024]{1,0:T(8,128)(2,1)} %wq.1, bf16[64,1024]{1,0:T(8,128)(2,1)} %wk.1, bf16[64,1024]{1,0:T(8,128)(2,1)} %wv.1, ...), custom_call_target="tpu_custom_call" | custom-call | tf_op jit(solution)/shard_map/pallas_call | solution.py:495
  71.0 1.9 %copy.9 = bf16[2,128,1024]{2,1,0:T(8,128)(2,1)} copy(bf16[2,128,1024]{2,1,0:T(8,128)(2,1)} %bitcast.4) | data formatting | bytes 1048576

commit v3 on v2

--- a/solution.py
+++ b/solution.py
@@ -113,7 +113,15 @@
 TN = (((0,), (0,)), ((), ()))
 F32 = jnp.float32
 BF16 = jnp.bfloat16
-ZFULL = (False, True, True)
+ZFULL = (False, False, True)
+XFIRST = (False, True, False)
+ORDER = (
+    "sw", "ox0", "oz0", "gw0", "ox1", "G0", "Gs", "x00", "oz1", "z0g1", "x10", "z1g1", "G1",
+    "gw1", "z1k1", "LNo", "LNp", "z1g2", "z1k2", "rG", "z0g2", "oz2", "z1g3", "z1k3", "rN",
+    "x01", "z0g3", "z2g1", "x03", "x02", "ox2", "z2g2", "act", "z2h1", "y1", "P0", "x21", "P1",
+    "z2g3", "x20", "P2", "y0", "GA0", "z2h2", "x22", "GA1", "x23", "A0", "z2h3", "A1", "B0",
+    "B1", "y2",
+)
 
 
 def kernel(
@@ -199,33 +207,45 @@
     def planes(ph):
         return (g, 1 - g) if ZFULL[ph] else (g,)
 
+    def along(ph, kind):
+        return (1 - x if kind == "k" else x), (1 - g if kind == "h" else g)
+
+    def start_z(ph, kind):
+        xi, e = along(ph, kind)
+        send_piece(ph, xi, e, z, up, has_up)
+        send_piece(ph, xi, e, z, down, has_down)
+
     def own_z(ph):
-        for e in planes(ph):
-            send_piece(ph, x, e, z, up, has_up)
-            send_piece(ph, x, e, z, down, has_down)
+        start_z(ph, "g")
+        if ZFULL[ph]:
+            start_z(ph, "h")
 
     def own_x(ph):
         send_piece(ph, x, g, z, xpeer)
 
-    def relay_z(ph, d):
+    def relay_z(ph, kind, d):
+        xi, e = along(ph, kind)
         for below in (True, False):
             here = (z >= d) if below else (z + d <= 3)
             on = jnp.logical_and(here, has_up if below else has_down)
             zi = lax.rem(z + (4 - d if below else d), 4)
-            for k, e in enumerate(planes(ph)):
-                @pl.when(here)
-                def _():
-                    got_piece(ph, x, e, zi)
-
-                send_piece(ph, x, e, zi, up if below else down, on)
-                if k == 0:
-                    send_piece(ph, x, e, zi, xpeer, here)
-                    if not ZFULL[ph]:
-                        send_piece(ph, x, e, zi, ypeer, here)
+
+            @pl.when(here)
+            def _():
+                got_piece(ph, xi, e, zi)
+
+            if d < 3:
+                send_piece(ph, xi, e, zi, up if below else down, on)
+            if kind == "g" and not XFIRST[ph]:
+                send_piece(ph, xi, e, zi, xpeer, here)
+            if kind == "k" or (kind == "g" and not ZFULL[ph]):
+                send_piece(ph, xi, e, zi, ypeer, here)
 
     def relay_x(ph, d):
         if d == 0:
             got_piece(ph, 1 - x, g, z)
+            if XFIRST[ph]:
+                start_z(ph, "k")
             send_piece(ph, 1 - x, g, z, ypeer)
             return
         for below in (True, False):
@@ -245,33 +265,35 @@
         for dz in (0, 1, 3, 2):
             got_piece(ph, 1 - x, 1 - g, lax.rem(z + dz, 4))
 
-    def steps(ph):
-        return [
-            functools.partial(relay_z, ph, 1),
-            functools.partial(relay_x, ph, 0),
-            functools.partial(relay_z, ph, 2),
-            functools.partial(relay_x, ph, 1),
-            functools.partial(relay_z, ph, 3),
-            functools.partial(relay_x, ph, 2),
-            functools.partial(relay_x, ph, 3),
-        ]
-
-    for d in locs[:2]:
-        d.wait()
-    own_z(0)
-    own_x(0)
-    for fr in range(2):
+    tasks = {}
+    for ph in range(3):
+        tasks["oz%d" % ph] = functools.partial(own_z, ph)
+        tasks["ox%d" % ph] = functools.partial(own_x, ph)
+        tasks["y%d" % ph] = functools.partial(rest, ph)
+        for d in range(4):
+            tasks["x%d%d" % (ph, d)] = functools.partial(relay_x, ph, d)
+            for kind in "ghk":
+                tasks["z%d%s%d" % (ph, kind, d)] = functools.partial(relay_z, ph, kind, d)
+
+    def sibling_weights():
+        for half in range(2):
+            for m in range(3):
+                col = pl.multiple_of(512 * half + 256 * (1 - c), 256)
+                send(
+                    weights[m].at[:, pl.ds(col, 256)], WQ.at[half, m, x, c, z], rs.at[m, half], sib
+                )
+
+    def got_weights(half):
+        for m in range(3):
+            got(WQ.at[half, m, x, 1 - c, z], rs.at[m, half])
+            locs[4 + 2 * m + half].wait()
+
+    def grad_peer(fr):
         send(gout_in.at[fr, 1 - x], XG.at[:, 2, fr], ra.at[0, 1, fr], xpeer)
-    for m in range(3):
-        for half in range(2):
-            col = pl.multiple_of(512 * half + 256 * (1 - c), 256)
-            send(
-                weights[m].at[:, pl.ds(col, 256)], WQ.at[half, m, x, c, z], rs.at[m, half], sib
-            )
-    for fr in range(2):
-        send(gout_in.at[fr, x], XG.at[:, 1, fr], ra.at[0, 0, fr], sib)
-    for d in locs[2:]:
-        d.wait()
+
+    def grad_sibling():
+        for fr in range(2):
+            send(gout_in.at[fr, x], XG.at[:, 1, fr], ra.at[0, 0, fr], sib)
 
     gains = gain[...]
 
@@ -284,34 +306,25 @@
         INV[fr, half] = jnp.broadcast_to(inverse, (64, 128)).reshape(4, 16, 128)
         return (unit * gains).astype(BF16).reshape(4, 16, 1024)
 
-    for fr in range(2):
-        NS[:, fr] = norm(1 - x, fr)
-    send(NS, XN.at[:, 2], ra.at[1, 1, 0], xpeer)
-    for m in range(3):
-        for half in range(2):
-            got(WQ.at[half, m, x, 1 - c, z], rs.at[m, half])
-    own_z(1)
-    own_x(1)
-    first = steps(0)
-    first[0]()
-    for fr in range(2):
-        XN[:, 0, fr] = norm(x, fr)
-        XG[:, 0, fr] = gout[fr, x]
-    send(XN.at[:, 0], XN.at[:, 1], ra.at[1, 0, 0], sib)
-    for step in first[1:4]:
-        step()
-    for fr in range(2):
-        got(XG.at[:, 2, fr], ra.at[0, 1, fr])
-    send(XG.at[:, 2], XG.at[:, 3], rb.at[0], sib)
-    for step in first[4:]:
-        step()
-    own_z(2)
-    own_x(2)
-    got(XN.at[:, 2], ra.at[1, 1, 0])
-    send(XN.at[:, 2], XN.at[:, 3], rb.at[1], sib)
-    second = steps(1)
-    for step in second:
-        step()
+    def norm_peer():
+        for fr in range(2):
+            NS[:, fr] = norm(1 - x, fr)
+        send(NS, XN.at[:, 2], ra.at[1, 1, 0], xpeer)
+
+    def norm_own():
+        for fr in range(2):
+            XN[:, 0, fr] = norm(x, fr)
+            XG[:, 0, fr] = gout[fr, x]
+        send(XN.at[:, 0], XN.at[:, 1], ra.at[1, 0, 0], sib)
+
+    def relay_grad():
+        for fr in range(2):
+            got(XG.at[:, 2, fr], ra.at[0, 1, fr])
+        send(XG.at[:, 2], XG.at[:, 3], rb.at[0], sib)
+
+    def relay_norm():
+        got(XN.at[:, 2], ra.at[1, 1, 0])
+        send(XN.at[:, 2], XN.at[:, 3], rb.at[1], sib)
 
     def weight(half, m):
         return WQ[half, m].reshape(1024, 256)
@@ -426,23 +439,27 @@
         got(XN.at[:, 1], ra.at[1, 0, 0])
         got(XG.at[:, 3], rb.at[0])
         got(XN.at[:, 3], rb.at[1])
-        rest(0)
-
-    work = [
-        [gather_rest, functools.partial(project_grad, 0)],
-        [functools.partial(project_grad, 1)],
-        [functools.partial(rest, 1), functools.partial(project_in, 0, 0)],
-        [functools.partial(project_in, 0, 1)],
-        [functools.partial(project_in, 0, 2)],
-        [functools.partial(attention, 0, 0)],
-        [functools.partial(attention, 0, 1), functools.partial(back_first, 0),
-         functools.partial(back_first, 1)],
-    ]
-    for step, tasks in zip(steps(2), work):
-        step()
-        for task in tasks:
-            task()
-    rest(2)
+
+    tasks["sw"] = sibling_weights
+    tasks["Gs"] = grad_sibling
+    tasks["LNp"] = norm_peer
+    tasks["LNo"] = norm_own
+    tasks["rG"] = relay_grad
+    tasks["rN"] = relay_norm
+    tasks["act"] = gather_rest
+    for k in range(2):
+        tasks["gw%d" % k] = functools.partial(got_weights, k)
+        tasks["G%d" % k] = functools.partial(grad_peer, k)
+        tasks["GA%d" % k] = functools.partial(project_grad, k)
+        tasks["A%d" % k] = functools.partial(attention, 0, k)
+        tasks["B%d" % k] = functools.partial(back_first, k)
+    for m in range(3):
+        tasks["P%d" % m] = functools.partial(project_in, 0, m)
+
+    for d in locs[:4]:
+        d.wait()
+    for name in ORDER:
+        tasks[name]()
     for m in range(3):
         project_in(1, m)
     attention(1, 0)

time: 73.1 us -> 60.6 us (0.83)
  Pallas kernels: 71 us -> 58.6 us
    pallas_call x1, Pallas kernels: 71 us -> 58.6 us  [fused(): pl.pallas_call(kernel, out_shape=jax.ShapeDtypeStruct(cut, BF16), in_spec...]
where the time goes in v3:
time: 60.6 us; the launch traced here: 60.5 us
  Pallas kernels  58.6 us (97%)
  local copies, waits for them, and re-layouts  1.87 us (3%)
    pallas_call x1, Pallas kernels, fused(): pl.pallas_call(kernel, out_shape=jax.ShapeDtypeStruct(cut, BF16), in_spec...  58.6 us
    unnamed x1, local copies, waits for them, and re-layouts  1.87 us

profile of v3, /device:TPU:0, one launch (start us, length us, event | category | flops | bytes accessed | tf_op | source)
XLA Modules:
  0.0 60.5 jit_solution(15556755839449032971)
XLA Ops:
  0.0 58.6 %shard_map.73 = bf16[2,2,4,16,1024]{4,3,2,1,0:T(8,128)(2,1)} custom-call(bf16[2,2,4,16,1024]{4,3,2,1,0:T(8,128)(2,1)} %bitcast.5, f32[1,1024]{1,0:T(1,128)} %bitcast.7, bf16[64,1024]{1,0:T(8,128)(2,1)} %wo.1, bf16[64,1024]{1,0:T(8,128)(2,1)} %wq.1, bf16[64,1024]{1,0:T(8,128)(2,1)} %wk.1, bf16[64,1024]{1,0:T(8,128)(2,1)} %wv.1, ...), custom_call_target="tpu_custom_call" | custom-call | tf_op jit(solution)/shard_map/pallas_call | solution.py:512
  58.6 1.9 %copy.9 = bf16[2,128,1024]{2,1,0:T(8,128)(2,1)} copy(bf16[2,128,1024]{2,1,0:T(8,128)(2,1)} %bitcast.4) | data formatting | bytes 1048576

commit v4 on v3

--- a/solution.py
+++ b/solution.py
@@ -115,6 +115,7 @@
 BF16 = jnp.bfloat16
 ZFULL = (False, False, True)
 XFIRST = (False, True, False)
+CHUNKS = ((0, 2), (2, 1), (3, 1))
 ORDER = (
     "sw", "ox0", "oz0", "gw0", "ox1", "G0", "Gs", "x00", "oz1", "z0g1", "x10", "z1g1", "G1",
     "gw1", "z1k1", "LNo", "LNp", "z1g2", "z1k2", "rG", "z0g2", "oz2", "z1g3", "z1k3", "rN",
@@ -127,7 +128,7 @@
 def kernel(
     tok_in, gain, wo, wq, wk, wv, gout_in, out,
     tok, gout, WO, WQ, XG, XN, NS, U, INV, QQ, KK, VV, DQ, DK, DV, GA, PA, PS, PO, SIBP, RS, RR,
-    loc, snd, rw, rs, ra, rb,
+    loc, snd, rw, rs, ra, rb, rc,
 ):
     g = lax.axis_index("groups")
     f = lax.axis_index("frame")
@@ -384,11 +385,10 @@
             DV[rows, cols] = jnp.where(low, dv[:128], dv[128:]).astype(BF16)
         return carry
 
-    def attention(half, ch):
-        lax.fori_loop(2 * ch, 2 * ch + 2, functools.partial(attend, half), 0)
-
-    def back(half, ch):
-        rows = pl.ds(256 * ch, 256)
+    def attention(half, start, count):
+        lax.fori_loop(start, start + count, functools.partial(attend, half), 0, unroll=True)
+
+    def back(half, rows):
         return (
             lax.dot_general(DQ[rows], weight(half, 0), NT, preferred_element_type=F32)
             + lax.dot_general(DK[rows], weight(half, 1), NT, preferred_element_type=F32)
@@ -396,42 +396,53 @@
         )
 
     def back_first(ch):
-        PA[ch] = back(0, ch)
+        rows = pl.ds(256 * ch, 256)
+        PA[rows] = back(0, rows)
+
+    def chunk(ch):
+        return pl.ds(*CHUNKS[ch])
 
     def back_last(ch):
-        part = (back(1, ch) + PA[ch]).reshape(2, 4, 2, 16, 1024)
-        PS[ch, :, 0] = part[:, 1]
-        PS[ch, :, 1] = part[:, 3]
-        send(PS.at[ch], SIBP.at[ch], rb.at[2 + ch], sib)
-        PO[ch, :, 0] = part[:, 0]
-        PO[ch, :, 1] = part[:, 2]
+        start, count = CHUNKS[ch]
+        rows = pl.ds(128 * start, 128 * count)
+        part = (back(1, rows) + PA[rows]).reshape(count, 4, 2, 16, 1024)
+        span = chunk(ch)
+        PS[span, 0] = part[:, 1]
+        PS[span, 1] = part[:, 3]
+        send(PS.at[span], SIBP.at[span], rc.at[0, ch], sib)
+        PO[span, 0] = part[:, 0]
+        PO[span, 1] = part[:, 2]
 
     def finish(ch, fr, half, grad_normed):
-        scaled = grad_normed.astype(F32).reshape(32, 1024) * gains
-        span = pl.ds(2 * ch, 2)
-        unit = U[fr, half, span].reshape(32, 1024)
-        inverse = INV[fr, half, span].reshape(32, 128)[:, :1]
+        count = CHUNKS[ch][1]
+        scaled = grad_normed.astype(F32).reshape(16 * count, 1024) * gains
+        span = chunk(ch)
+        unit = U[fr, half, span].reshape(16 * count, 1024)
+        inverse = INV[fr, half, span].reshape(16 * count, 128)[:, :1]
         grad_in = inverse * (
             scaled
             - jnp.mean(scaled, axis=-1, keepdims=True)
             - unit * jnp.mean(scaled * unit, axis=-1, keepdims=True)
         )
-        base = gout[fr, half, span].astype(F32).reshape(32, 1024)
-        out[fr, half, span] = (base + grad_in).astype(BF16).reshape(2, 16, 1024)
+        base = gout[fr, half, span].astype(F32).reshape(16 * count, 1024)
+        out[fr, half, span] = (base + grad_in).astype(BF16).reshape(count, 16, 1024)
 
     def combine(ch):
-        got(SIBP.at[ch], rb.at[2 + ch])
-        RS[ch] = (PO[ch, :, 1] + SIBP[ch, :, 1]).astype(BF16)
-        send(RS.at[ch], RR.at[ch], rb.at[4 + ch], xpeer)
+        span = chunk(ch)
+        got(SIBP.at[span], rc.at[0, ch])
+        RS[span] = (PO[span, 1] + SIBP[span, 1]).astype(BF16)
+        send(RS.at[span], RR.at[span], rc.at[1, ch], xpeer)
 
     def finish_own(ch):
-        for fr in range(2):
-            finish(ch, fr, x, (PO[ch, :, 0, fr] + SIBP[ch, :, 0, fr]).astype(BF16))
+        span = chunk(ch)
+        for fr in range(2):
+            finish(ch, fr, x, (PO[span, 0, fr] + SIBP[span, 0, fr]).astype(BF16))
 
     def finish_peer(ch):
-        got(RR.at[ch], rb.at[4 + ch])
-        for fr in range(2):
-            finish(ch, fr, 1 - x, RR[ch, :, fr])
+        span = chunk(ch)
+        got(RR.at[span], rc.at[1, ch])
+        for fr in range(2):
+            finish(ch, fr, 1 - x, RR[span, fr])
 
     def gather_rest():
         for fr in range(2):
@@ -451,7 +462,7 @@
         tasks["gw%d" % k] = functools.partial(got_weights, k)
         tasks["G%d" % k] = functools.partial(grad_peer, k)
         tasks["GA%d" % k] = functools.partial(project_grad, k)
-        tasks["A%d" % k] = functools.partial(attention, 0, k)
+        tasks["A%d" % k] = functools.partial(attention, 0, 2 * k, 2)
         tasks["B%d" % k] = functools.partial(back_first, k)
     for m in range(3):
         tasks["P%d" % m] = functools.partial(project_in, 0, m)
@@ -462,16 +473,18 @@
         tasks[name]()
     for m in range(3):
         project_in(1, m)
-    attention(1, 0)
-    back_last(0)
-    attention(1, 1)
-    combine(0)
-    back_last(1)
-    finish_own(0)
-    combine(1)
-    finish_own(1)
-    finish_peer(0)
-    finish_peer(1)
+    last = len(CHUNKS) - 1
+    for ch in range(last + 1):
+        attention(1, *CHUNKS[ch])
+        if ch > 0:
+            combine(ch - 1)
+        back_last(ch)
+        if ch > 0:
+            finish_own(ch - 1)
+    combine(last)
+    finish_own(last)
+    for ch in range(last + 1):
+        finish_peer(ch)
 
     for d, when in sends:
         if when is None:
@@ -498,16 +511,17 @@
         pltpu.VMEM((2, 2, 4, 16, 128), F32),
     ]
     scratch += [pltpu.VMEM((512, 256), BF16)] * 6
-    scratch += [pltpu.VMEM((512, 512), BF16), pltpu.VMEM((2, 256, 1024), F32)]
-    scratch += [pltpu.VMEM((2, 2, 2, 2, 16, 1024), F32)] * 3
-    scratch += [pltpu.VMEM((2, 2, 2, 16, 1024), BF16)] * 2
+    scratch += [pltpu.VMEM((512, 512), BF16), pltpu.VMEM((512, 1024), F32)]
+    scratch += [pltpu.VMEM((4, 2, 2, 16, 1024), F32)] * 3
+    scratch += [pltpu.VMEM((4, 2, 16, 1024), BF16)] * 2
     scratch += [
         pltpu.SemaphoreType.DMA((10,)),
         pltpu.SemaphoreType.DMA((128,)),
         pltpu.SemaphoreType.DMA((3, 2, 2, 4)),
         pltpu.SemaphoreType.DMA((3, 2)),
         pltpu.SemaphoreType.DMA((2, 2, 2)),
-        pltpu.SemaphoreType.DMA((6,)),
+        pltpu.SemaphoreType.DMA((2,)),
+        pltpu.SemaphoreType.DMA((2, len(CHUNKS))),
     ]
     result = pl.pallas_call(
         kernel,

time: 60.6 us -> 60.2 us (level)
  no operation moved by 1% of the time
where the time goes in v4:
time: 60.2 us; the launch traced here: 60 us
  Pallas kernels  58.2 us (97%)
  local copies, waits for them, and re-layouts  1.87 us (3%)
    pallas_call x1, Pallas kernels, fused(): pl.pallas_call(kernel, out_shape=jax.ShapeDtypeStruct(cut, BF16), in_spec...  58.2 us
    unnamed x1, local copies, waits for them, and re-layouts  1.87 us

profile of v4, /device:TPU:0, one launch (start us, length us, event | category | flops | bytes accessed | tf_op | source)
XLA Modules:
  0.0 60.0 jit_solution(4925879546297799790)
XLA Ops:
  0.0 58.2 %shard_map.73 = bf16[2,2,4,16,1024]{4,3,2,1,0:T(8,128)(2,1)} custom-call(bf16[2,2,4,16,1024]{4,3,2,1,0:T(8,128)(2,1)} %bitcast.5, f32[1,1024]{1,0:T(1,128)} %bitcast.7, bf16[64,1024]{1,0:T(8,128)(2,1)} %wo.1, bf16[64,1024]{1,0:T(8,128)(2,1)} %wq.1, bf16[64,1024]{1,0:T(8,128)(2,1)} %wk.1, bf16[64,1024]{1,0:T(8,128)(2,1)} %wv.1, ...), custom_call_target="tpu_custom_call" | custom-call | tf_op jit(solution)/shard_map/pallas_call | solution.py:526
  58.2 1.9 %copy.9 = bf16[2,128,1024]{2,1,0:T(8,128)(2,1)} copy(bf16[2,128,1024]{2,1,0:T(8,128)(2,1)} %bitcast.4) | data formatting | bytes 1048576
